TPU v7x, 32 devices: a whole 2x2x4 slice. The times are simulated.
32 devices in a mesh: ctx: 8 (over z, y), head: 4 (over x, core).
Axes of the slice: x: 2, y: 2, z: 4, core: 2. Of those that a mesh axis runs over, the one named last changes fastest.
Arguments:
- queries: bfloat16 [4096, 2048], P('ctx', 'head'), may hold values from -4.5 to 4.5
- keys: bfloat16 [4096, 1024], P('ctx', 'head'), may hold values from -4.5 to 4.5
- values: bfloat16 [4096, 1024], P('ctx', 'head'), may hold values from -4.5 to 4.5
- offsets: int32 [8], P('ctx'), may hold values from 0 to 512, as said below
- gate_logits: float32 [16], P('head'), may hold values from -2 to 2
- out_weight: bfloat16 [2048, 2048], P('head'), may hold values from -0.125 to 0.125
- grad_mixed: bfloat16 [4096, 2048], P('ctx', 'head'), may hold values from -6 to 6
Outputs:
- mixed: bfloat16 [4096, 2048], P('ctx', 'head')
- grad_queries: float32 [4096, 2048], P('ctx', 'head')
- grad_keys: float32 [4096, 1024], P('ctx', 'head')
- grad_values: float32 [4096, 1024], P('ctx', 'head')
- grad_weight: float32 [2048, 2048], P('head', 'ctx')
- grad_gates: float32 [16], P('head')
Inputs may be any that keep to these rules, and one draw needn't show every extreme that they name: `offsets`: entry s is 512 where segment s continues the document of the segment before it, else the position within segment s at which a new document begins.
All inputs are finite; a program needn't handle non-finite values.
Results may differ from a plain program's by a relative error of at most 0.0064.
Values may be sent and summed in bfloat16 or wider, within the bound.
A program may use at most 64 MiB of HBM per device.

v0:
```python
import jax
import jax.numpy as jnp
from jax import lax
from jax.sharding import PartitionSpec as P

HEAD_DIM = 128
SEG = 512


highest = lax.Precision.HIGHEST


def carried_in(value, axis, join, neutral, backward):
    count, mine = (lax.axis_size(axis), lax.axis_index(axis))
    pieces = jax.tree.map(lambda part: lax.all_gather(part, axis), value)
    if backward:
        pieces = jax.tree.map(lambda part: part[::-1], pieces)
        mine = count - 1 - mine
    running = jax.tree.map(
        lambda part, zero: jnp.full_like(part, 0) + jnp.asarray(zero, part.dtype), value, neutral
    )

    def hop(position, running):
        longer = join(running, jax.tree.map(lambda part: part[position], pieces))
        return jax.tree.map(lambda new, old: jnp.where(position < mine, new, old), longer, running)

    return lax.fori_loop(0, count - 1, hop, running)


def feature(inputs):
    return jnp.where(inputs > 0, inputs + 1.0, jnp.exp(jnp.minimum(inputs, 0.0)))


def feature_slope(inputs):
    return jnp.where(inputs > 0, 1.0, jnp.exp(jnp.minimum(inputs, 0.0)))


def compose(earlier, later):
    return (
        later[2][:, None, None] * earlier[0] + later[0],
        later[2][:, None] * earlier[1] + later[1],
        earlier[2] * later[2],
    )


def segment_element(memory, totals, factor, segment):
    return (memory[segment], totals[segment], factor)


def body(queries, keys, values, offsets, gate_logits, out_weight, grad_mixed):
    tokens = queries.shape[0]
    head_count = queries.shape[1] // HEAD_DIM
    groups = keys.shape[1] // HEAD_DIM
    repeat = head_count // groups
    segments = tokens // SEG
    score_scale = HEAD_DIM ** (-0.5)
    query_blocks = queries.reshape(segments, SEG, groups, repeat, HEAD_DIM)
    key_blocks = keys.reshape(segments, SEG, groups, HEAD_DIM)
    value_blocks = values.reshape(segments, SEG, groups, HEAD_DIM)
    query_float = query_blocks.astype(jnp.float32)
    key_float = key_blocks.astype(jnp.float32)
    value_float = value_blocks.astype(jnp.float32)
    query_feat = feature(query_float)
    key_feat = feature(key_float)
    position = jnp.arange(SEG)
    retain = (position[None, :] < offsets[:, None]).astype(jnp.float32)
    start_cut = jnp.where(offsets == SEG, 0, offsets)
    counted = (position[None, :] >= start_cut[:, None]).astype(jnp.float32)
    carry_factor = (offsets == SEG).astype(jnp.float32)
    counted_feat = key_feat * counted[:, :, None, None]
    delta_memory = jnp.einsum("sjgd,sjge->sgde", counted_feat, value_float, precision=highest)
    delta_totals = jnp.sum(counted_feat, axis=1)
    identity = (
        jnp.zeros((groups, HEAD_DIM, HEAD_DIM), jnp.float32),
        jnp.zeros((groups, HEAD_DIM), jnp.float32),
        jnp.ones((1,), jnp.float32),
    )
    device_element = identity
    segment = 0
    device_element = compose(
        device_element, segment_element(delta_memory, delta_totals, carry_factor, segment)
    )
    incoming = carried_in(device_element, "ctx", compose, identity, False)
    running = incoming
    segment = 0
    memory_list = [running[0]]
    totals_list = [running[1]]
    memory_in = jnp.stack(memory_list)
    totals_in = jnp.stack(totals_list)
    retained_feat = query_feat * retain[:, :, None, None, None]
    numerator = jnp.einsum("sigrd,sgde->sigre", retained_feat, memory_in, precision=highest)
    denominator = 1.0 + jnp.einsum("sigrd,sgd->sigr", retained_feat, totals_in, precision=highest)
    recall = numerator / denominator[..., None]
    scores = (
        jnp.einsum(
            "sigrd,sjgd->sgrij", query_blocks, key_blocks, preferred_element_type=jnp.float32
        )
        * score_scale
    )
    later_doc = position[None, :] >= offsets[:, None]
    allowed = (position[None, None, :] <= position[None, :, None]) & (
        later_doc[:, :, None] == later_doc[:, None, :]
    )
    scores = jnp.where(allowed[:, None, None], scores, -1e30)
    scaled_exp = jnp.exp(scores - jnp.max(scores, axis=-1, keepdims=True))
    weights = scaled_exp / jnp.sum(scaled_exp, axis=-1, keepdims=True)
    weights_low = weights.astype(jnp.bfloat16)
    attend = jnp.einsum(
        "sgrij,sjgd->sigrd", weights_low, value_blocks, preferred_element_type=jnp.float32
    )
    sigmoid_gate = jax.nn.sigmoid(gate_logits).reshape(groups, repeat)
    mixing = sigmoid_gate[None, None, :, :, None]
    output = (mixing * recall + (1.0 - mixing) * attend).astype(jnp.bfloat16)
    out_flat = output.reshape(tokens, head_count * HEAD_DIM)
    gathered = lax.all_gather(out_flat, "head", axis=1, tiled=True)
    weight_cols = lax.all_to_all(out_weight, "head", split_axis=1, concat_axis=0, tiled=True)
    mixed = jnp.dot(gathered, weight_cols, preferred_element_type=jnp.float32).astype(jnp.bfloat16)
    cotangent = lax.all_gather(grad_mixed, "head", axis=1, tiled=True)
    grad_output = lax.dot_general(
        cotangent, out_weight, (((1,), (1,)), ((), ())), preferred_element_type=jnp.float32
    ).astype(jnp.bfloat16)
    weight_terms = lax.dot_general(
        out_flat, cotangent, (((0,), (0,)), ((), ())), preferred_element_type=jnp.float32
    )
    grad_weight = lax.psum_scatter(weight_terms, "ctx", scatter_dimension=1, tiled=True)
    grad_blocks = grad_output.reshape(segments, SEG, groups, repeat, HEAD_DIM)
    grad_float = grad_blocks.astype(jnp.float32)
    gate_slope = sigmoid_gate * (1.0 - sigmoid_gate)
    gate_terms = (jnp.sum(grad_float * (recall - attend), axis=(0, 1, 4)) * gate_slope).reshape(
        head_count
    )
    grad_recall = mixing * grad_float
    complement = (1.0 - sigmoid_gate)[None, :, :, None, None]
    grad_probs = complement * jnp.einsum(
        "sigrd,sjgd->sgrij", grad_blocks, value_blocks, preferred_element_type=jnp.float32
    )
    grad_scores = (
        weights * (grad_probs - jnp.sum(grad_probs * weights, axis=-1, keepdims=True)) * score_scale
    )
    grad_low = grad_scores.astype(jnp.bfloat16)
    grad_query = jnp.einsum(
        "sgrij,sjgd->sigrd", grad_low, key_blocks, preferred_element_type=jnp.float32
    )
    grad_key = jnp.einsum(
        "sgrij,sigrd->sjgd", grad_low, query_blocks, preferred_element_type=jnp.float32
    )
    value_terms = jnp.einsum(
        "sgrij,sigrd->sjgrd", weights_low, grad_blocks, preferred_element_type=jnp.float32
    )
    grad_value = jnp.sum(value_terms * (1.0 - sigmoid_gate)[None, None, :, :, None], axis=3)
    grad_numer = grad_recall / denominator[..., None]
    grad_denom = -jnp.sum(grad_recall * numerator, axis=-1) / (denominator * denominator)
    grad_feat = retain[:, :, None, None, None] * (
        jnp.einsum("sigre,sgde->sigrd", grad_numer, memory_in, precision=highest)
        + grad_denom[..., None] * totals_in[:, None, :, None, :]
    )
    grad_memory = jnp.einsum("sigrd,sigre->sgde", retained_feat, grad_numer, precision=highest)
    grad_totals = jnp.einsum("sigr,sigrd->sgd", grad_denom, retained_feat, precision=highest)
    grad_queries = (grad_query + grad_feat * feature_slope(query_float)).reshape(
        tokens, head_count * HEAD_DIM
    )
    device_grad = identity
    for segment in reversed(range(segments)):
        device_grad = compose(
            device_grad, segment_element(grad_memory, grad_totals, carry_factor, segment)
        )
    flowing = carried_in(device_grad, "ctx", compose, identity, True)
    running = flowing
    flow_list = []
    flow_totals_list = []
    for segment in reversed(range(segments)):
        flow_list.append(running[0])
        flow_totals_list.append(running[1])
        running = compose(running, segment_element(grad_memory, grad_totals, carry_factor, segment))
    flow_memory = jnp.stack(flow_list[::-1])
    flow_totals = jnp.stack(flow_totals_list[::-1])
    counted_wide = counted[:, :, None, None]
    grad_key_feat = counted_wide * (
        jnp.einsum("sjge,sgde->sjgd", value_float, flow_memory, precision=highest)
        + flow_totals[:, None, :, :]
    )
    grad_keys = (grad_key + grad_key_feat * feature_slope(key_float)).reshape(
        tokens, groups * HEAD_DIM
    )
    grad_value_mem = counted_wide * jnp.einsum(
        "sjgd,sgde->sjge", key_feat, flow_memory, precision=highest
    )
    grad_values = (grad_value + grad_value_mem).reshape(tokens, groups * HEAD_DIM)
    grad_gates = lax.psum(gate_terms, "ctx")
    return (mixed, grad_queries, grad_keys, grad_values, grad_weight, grad_gates)


def solution(mesh):
    placed = (
        P("ctx", "head"),
        P("ctx", "head"),
        P("ctx", "head"),
        P("ctx"),
        P("head"),
        P("head", None),
        P("ctx", "head"),
    )
    return jax.shard_map(
        body,
        mesh=mesh,
        in_specs=placed,
        out_specs=(
            P("ctx", "head"),
            P("ctx", "head"),
            P("ctx", "head"),
            P("ctx", "head"),
            P("head", "ctx"),
            P("head"),
        ),
        check_vma=False,
    )
```

profile of v0, /device:TPU:13, one launch (start us, length us, event | category | flops | bytes accessed | tf_op | source)
XLA Modules:
  0.0 245.1 jit_solution(16194960116923436702)
XLA Ops:
  8.0 2.4 fusion.75
  12.2 1.9 fusion.58
  14.1 1.7 reshape.411
  16.3 11.3 %all_gather.30 = f32[8,2,128]{2,1,0:T(2,128)S(1)} all-gather(f32[1,2,128]{2,1,0:T(2,128)S(1)} %bitcast.306), channel_id=1, replica_groups=mesh['ctx'=8,'head'=4] {'ctx'}, dimensions={0}, use_global_device_ids=true | all-gather | bytes 9216 | tf_op jit(solution)/shard_map/all_gather | solution.py:15
  29.1 18.1 %all-reduce = f32[8]{0:T(128)S(1)} all-reduce(f32[8]{0:T(128)S(1)} %convert_dynamic-update-slice_fusion), channel_id=2, replica_groups=mesh['ctx'=8,'head'=4] {'ctx'}, use_global_device_ids=true, to_apply=%add | all-reduce | flops 8 | bytes 64
  47.3 2.5 %all-gather.14.cloned.1.call-done = f32[16,128,128]{2,1,0:T(8,128)} async-done(((f32[2,128,128]{2,1,0:T(8,128)}), f32[16,128,128]{2,1,0:T(8,128)}) %all-gather.14.cloned.1.call-update) | async-done | bytes 1048592 | tf_op jit(solution)/shard_map/all_gather | solution.py:15
  49.8 20.0 %while.32 = (s32[]{:T(128)}, f32[2,128,128]{2,1,0:T(8,128)S(1)}, f32[2,128]{1,0:T(2,128)S(1)}, s32[]{:T(128)}, f32[8,1]{0,1:T(1,128)S(1)}, /*index=5*/f32[8,2,12...) while((s32[]{:T(128)}, f32[2,128,128]{2,1,0:T(8,128)S(1)}, ...), condition=%wide.region_2.3_spmd.clone, body=%wide.region_1.2_spmd.clone.sunk | while | flops 132100 | bytes 396431 | solution.py:27
  69.8 1.8 convolution_add_fusion
  72.0 3.7 %all-gather.12.cloned.1.call-done = bf16[512,2048]{1,0:T(8,128)(2,1)} async-done(((bf16[512,512]{1,0:T(8,128)(2,1)}), bf16[512,2048]{1,0:T(8,128)(2,1)}) %all-gather.12.cloned.1.call-update) | async-done | bytes 2097168 | tf_op jit(solution)/shard_map/all_gather | solution.py:118
  75.7 3.5 %convolution_convert_fusion = bf16[512,512]{0,1:T(8,128)(2,1)S(1)} fusion(bf16[512,2048]{1,0:T(8,128)(2,1)} %all-gather.12.cloned.1.call-done, bf16[512,2048]{1,0:T(8,128)(2,1)} %param.16), kind=kOutput, calls=%fused_computation.43 | convolution fusion | flops 1074003968 | bytes 4718592 | tf_op jit(solution)/shard_map/dot_general | solution.py:119
  79.2 2.2 convolution_bitcast_fusion.6
  84.9 2.7 %fusion.42 = (f32[2,2]{1,0:T(2,128)S(1)}, f32[512,2,2]{0,2,1:T(2,128)S(1)}, bf16[1,512,2,2,128]{1,4,3,2,0:T(8,128)(2,1)}) fusion(bf16[1,512,2,2,128]{1,4,3,2,0:T(8,128)(2,1)S(1)} %bitcast.311, f32[1,512,2,2,128]{1,4,3,2,0:T(8,128)S(1)} %convolution_bitcast_fusion.2, f32[512,2,2]{0,2,1:T(2,128)S(1)} %bitcast_bitcast_fusion, f32[2,2]{1,0:T(2,128)S(1)} %mul.296, ...), kind=kOutput, calls=%fused_computation.62 | convolution fusion | flops 276822016 | bytes 6848560 | tf_op jit(solution)/shard_map/sgrij,sjgd->sigrd/dot_general | solution.py:108
  87.6 2.6 %copy.103 = bf16[512,2048]{0,1:T(8,128)(2,1)} copy(bf16[512,2048]{1,0:T(8,128)(2,1)S(1)} %copy-done.5) | data formatting | bytes 4194304 | tf_op args[5]
  90.1 4.4 %all-to-all-start = ((bf16[512,4,512]{0,2,1:T(8,128)(2,1)}), bf16[512,4,512]{0,2,1:T(8,128)(2,1)S(1)}, u32[]{:S(2)}, u32[]{:S(2)}) async-start(bf16[512,4,512]{0,2,1:T(8,128)(2,1)} %bitcast.284), calls=%async_computation | async-start | bytes 4194304 | tf_op jit(solution)/shard_map/all_to_all | solution.py:116
  95.1 2.0 copy.115
  97.2 5.0 %fusion.117 = f32[512,2048]{1,0:T(8,128)} fusion(bf16[512,512]{0,1:T(8,128)(2,1)} %bitcast.295, bf16[512,2048]{1,0:T(8,128)(2,1)} %all-gather.12.cloned.1.call-done), kind=kOutput, calls=%fused_computation.148 | convolution fusion | flops 1073741824 | bytes 6815744 | tf_op jit(solution)/shard_map/dot_general | solution.py:122
  102.2 2.2 fusion.39
  104.4 2.5 %copy.110 = f32[512,512]{0,1:T(8,128)} copy(f32[512,512]{1,0:T(8,128)} %fusion.39) | data formatting | bytes 2097152 | tf_op jit(solution)/shard_map/jit(_where)/select_n | solution.py:35
  107.0 12.4 %all-to-all-done = bf16[512,4,512]{0,2,1:T(8,128)(2,1)S(1)} async-done(((bf16[512,4,512]{0,2,1:T(8,128)(2,1)}), bf16[512,4,512]{0,2,1:T(8,128)(2,1)S(1)}, u32[]{:S(2)}, u32[]{:S(2)}) %all-to-all-start) | async-done | bytes 2097184 | tf_op jit(solution)/shard_map/all_to_all | solution.py:116
  119.5 2.4 copy.104
  121.9 14.5 %psum.7 = f32[4]{0:T(128)} all-reduce(f32[4]{0:T(128)S(1)} %fusion.102), channel_id=1, replica_groups=mesh['ctx'=8,'head'=4] {'ctx'}, use_global_device_ids=true, to_apply=%region_12.13 | all-reduce | flops 4 | bytes 32 | tf_op jit(solution)/shard_map/psum | solution.py:189
  137.6 14.2 %all-gather.4 = f32[8,2,128]{2,1,0:T(2,128)S(1)} all-gather(f32[1,2,128]{2,1,0:T(2,128)S(1)} %bitcast.307), channel_id=5, replica_groups=mesh['ctx'=8,'head'=4] {'ctx'}, dimensions={0}, use_global_device_ids=true | all-gather | bytes 9216 | tf_op jit(solution)/shard_map/all_gather | solution.py:15
  151.7 4.3 %multiply_reduce_fusion = (f32[2,2,512]{2,1,0:T(2,128)S(1)}, f32[2,512,2,512]{1,3,2,0:T(8,128)S(1)}) fusion(f32[2,2]{1,0:T(2,128)S(1)} %broadcast_subtract_fusion, f32[2,2,512]{2,1,0:T(2,128)S(1)} %fusion.6, f32[2,2,512]{2,1,0:T(2,128)S(1)} %get-tuple-element.365, f32[2,512,512,2]{2,1,3,0:T(8,128)} %copy-done, pred[512,512]{0,1:T(8,128)(4,1)S(1)} %fusion.46, ...), kind=kOutput, calls=%fused_computation.14 | convolution fusion | flops 275773440 | bytes 9461776 | tf_op jit(solution)/shard_map/sigrd,sjgd->sgrij/dot_general | solution.py:134
  158.2 2.4 fusion.23
  160.6 2.5 %copy.118 = f32[512,512]{1,0:T(8,128)} copy(f32[512,512]{0,1:T(8,128)} %bitcast.298) | data formatting | bytes 2097152
  163.1 4.6 %fusion.27 = f32[2,128,512]{2,1,0:T(8,128)} fusion(bf16[512,2,2,128]{0,3,2,1:T(8,128)(2,1)} %bitcast.310, f32[2,2]{1,0:T(2,128)S(1)} %broadcast_subtract_fusion, f32[2,2,512]{2,1,0:T(2,128)S(1)} %fusion.6, f32[2,2,512]{2,1,0:T(2,128)S(1)} %get-tuple-element.365, f32[2,512,512,2]{2,1,3,0:T(8,128)} %copy-done, pred[512,512]{0,1:T(8,128)(4,1)S(1)} %fusion.46), kind=kOutput, calls=%fused_computation.45 | convolution fusion | flops 274071552 | bytes 5521424 | tf_op jit(solution)/shard_map/sgrij,sigrd->sjgrd/dot_general | solution.py:147
  167.7 2.4 rev.10
  170.2 24.4 %while.33 = (s32[]{:T(128)}, f32[2,128,128]{2,1,0:T(8,128)S(1)}, f32[2,128]{1,0:T(2,128)S(1)}, s32[]{:T(128)}, f32[8,1]{0,1:T(1,128)}, /*index=5*/f32[8,2,128,12...) while((s32[]{:T(128)}, f32[2,128,128]{2,1,0:T(8,128)S(1)}, f32[2,128]{1,0:T(2,128)S(1)}, ...), condition=%wide.region_8.9_spmd.clone, body=%wide.region_7.8_spmd.clone.sunk | while | flops 132100 | bytes 396431 | solution.py:27
  194.6 2.5 %fusion.37 = f32[1,512,2,128]{1,3,2,0:T(8,128)} fusion(f32[2,128,128]{2,1,0:T(8,128)S(1)} %get-tuple-element.258, f32[2,128,512]{2,1,0:T(8,128)} %fusion.27, f32[512]{0:T(512)S(1)} %fusion.100, bf16[512,256]{1,0:T(8,128)(2,1)S(1)} %copy-done.2), kind=kOutput, calls=%fused_computation.56 | convolution fusion | flops 202244096 | bytes 1443840 | tf_op jit(solution)/shard_map/sjgd,sgde->sjge/dot_general | solution.py:185
  197.2 2.0 copy.120
  202.4 4.3 %convolution_convert_fusion.1 = bf16[512,512]{1,0:T(8,128)(2,1)} fusion(bf16[512,2048]{0,1:T(8,128)(2,1)} %all-gather.10.cloned.1.call-done, bf16[2048,512]{1,0:T(8,128)(2,1)} %bitcast.282), kind=kOutput, calls=%fused_computation.44 | convolution fusion | flops 1074003968 | bytes 4718592 | tf_op jit(solution)/shard_map/dot_general | solution.py:117
  206.7 31.9 %reduce-scatter.2.cloned.1.call-done = f32[512,256]{1,0:T(8,128)} async-done(((f32[512,2048]{1,0:T(8,128)}), f32[512,256]{1,0:T(8,128)}) %reduce-scatter.2.cloned.1.call-update) | async-done | bytes 524304 | tf_op jit(solution)/shard_map/reduce_scatter | solution.py:125
  (113 shorter events, 59.0 us)
Async XLA Ops:
  7.2 20.5 %copy-start.12 = (u32[32]{0:T(128)S(1)}, u32[32]{0:T(128)}, u32[]{:S(2)}) copy-start(u32[32]{0:T(128)} %constant.86) | copy-start | bytes 388
  7.2 8.9 %copy-start.3 = (bf16[512,512]{1,0:T(8,128)(2,1)S(1)}, bf16[512,512]{1,0:T(8,128)(2,1)}, u32[]{:S(2)}) copy-start(bf16[512,512]{1,0:T(8,128)(2,1)} %param.11) | copy-start | bytes 1572868
  7.2 40.0 %copy-start.8 = (f32[4]{0:T(128)S(1)}, f32[4]{0:T(128)}, u32[]{:S(2)}) copy-start(f32[4]{0:T(128)} %param.15) | copy-start | bytes 52
  7.2 42.6 %all-gather.14.cloned.1.call-start = ((), (), s32[]{:S(2)}) async-start(), calls=%async_computation.5 | async-start | bytes 1179648 | tf_op jit(solution)/shard_map/all_gather | solution.py:15
  10.4 65.3 %all-gather.12.cloned.1.call-start = ((), (), s32[]{:S(2)}) async-start(), calls=%async_computation.3 | async-start | bytes 2621440 | tf_op jit(solution)/shard_map/all_gather | solution.py:118
  11.1 156.6 %all-gather.16.cloned.1.call-start = ((), (), s32[]{:S(2)}) async-start(), calls=%async_computation.6 | async-start | bytes 1179648 | tf_op jit(solution)/shard_map/all_gather | solution.py:15
  79.2 3.4 %copy-start.9 = (bf16[512,512]{0,1:T(8,128)(2,1)}, bf16[512,512]{0,1:T(8,128)(2,1)S(1)}, u32[]{:S(2)}) copy-start(bf16[512,512]{0,1:T(8,128)(2,1)S(1)} %convolution_convert_fusion) | copy-start | bytes 1572868
  81.4 121.0 %all-gather.10.cloned.1.call-start = ((), (), s32[]{:S(2)}) async-start(), calls=%async_computation.2 | async-start | bytes 2621440 | tf_op jit(solution)/shard_map/all_gather | solution.py:115
  82.6 4.9 %copy-start = (f32[2,512,512,2]{2,1,3,0:T(8,128)}, f32[2,512,512,2]{2,1,3,0:T(8,128)S(1)}, u32[]{:S(2)}) copy-start(f32[2,512,512,2]{2,1,3,0:T(8,128)S(1)} %get-tuple-element.366) | copy-start | bytes 12582916
  82.6 2.2 copy-start.7
  82.6 2.2 copy-start.10
  84.9 2.7 %copy-start.5 = (bf16[512,2048]{1,0:T(8,128)(2,1)S(1)}, bf16[512,2048]{1,0:T(8,128)(2,1)}, u32[]{:S(2)}) copy-start(bf16[512,2048]{1,0:T(8,128)(2,1)} %param.16) | copy-start | bytes 6291460
  90.1 29.3 %all-to-all-start = ((bf16[512,4,512]{0,2,1:T(8,128)(2,1)}), bf16[512,4,512]{0,2,1:T(8,128)(2,1)S(1)}, u32[]{:S(2)}, u32[]{:S(2)}) async-start(bf16[512,4,512]{0,2,1:T(8,128)(2,1)} %bitcast.284), calls=%async_computation | async-start | bytes 4194304 | tf_op jit(solution)/shard_map/all_to_all | solution.py:116
  94.5 144.1 %reduce-scatter.2.cloned.1.call-start = ((), (), s32[]{:S(2)}) async-start(), calls=%async_computation.4 | async-start | bytes 4718592 | tf_op jit(solution)/shard_map/reduce_scatter | solution.py:125
  151.7 4.3 %copy-start.1 = (f32[2,512,512,2]{2,1,3,0:T(8,128)S(1)}, f32[2,512,512,2]{2,1,3,0:T(8,128)}, u32[]{:S(2)}) copy-start(f32[2,512,512,2]{2,1,3,0:T(8,128)} %copy-done) | copy-start | bytes 12582916
  156.0 2.1 copy-start.6
  156.0 2.1 copy-start.11
  167.7 26.9 %copy-start.2 = (bf16[512,256]{1,0:T(8,128)(2,1)S(1)}, bf16[512,256]{1,0:T(8,128)(2,1)}, u32[]{:S(2)}) copy-start(bf16[512,256]{1,0:T(8,128)(2,1)} %param.12) | copy-start | bytes 786436
  167.7 31.5 %copy-start.4 = (f32[512,256]{0,1:T(8,128)S(1)}, f32[512,256]{0,1:T(8,128)}, u32[]{:S(2)}) copy-start(f32[512,256]{0,1:T(8,128)} %copy.115) | copy-start | bytes 1572868
Sparse Core Ops, SparseCore 0:
  10.7 39.0 all-gather.13
  51.4 24.2 all-gather.11
  81.5 38.6 all-gather.15
  122.2 24.2 all-gather.9
  150.6 87.9 reduce-scatter.1
where the time goes:
time: 248 us; the launch traced here: 245 us
  blocking collectives  58.1 us (23%)
  waiting for transfers between devices  51.3 us (21%)
  matrix products  41.6 us (17%)
  other arithmetic  39.4 us (16%)
  local copies, waits for them, and re-layouts  35 us (14%)
  between operations  14.8 us (6%)
  starting transfers between devices  4.72 us (2%)
    reduce_scatter x1, waiting for transfers between devices, body(): lax.psum_scatter(weight_terms, 'ctx', scatter_dimension=1, tiled=True)  31.9 us
    select_n x28, other arithmetic, hop(): jnp.where(position < mine, new, old)  31.7 us
    all_gather x2, blocking collectives, carried_in(): pieces = jax.tree.map(lambda part: lax.all_gather(part, axis), value)  25.5 us
    unnamed x1, blocking collectives  18.1 us
    psum x1, blocking collectives, body(): grad_gates = lax.psum(gate_terms, 'ctx')  14.5 us
    dynamic_slice x14, local copies, waits for them, and re-layouts, hop(): longer = join(running, jax.tree.map(lambda part: part[position], pieces))  12.6 us
    all_to_all x1, waiting for transfers between devices, body(): lax.all_to_all(out_weight, 'head', split_axis=1, concat_axis=0, tiled=True)  12.4 us
    unnamed x34, local copies, waits for them, and re-layouts  9.73 us
  transfers between devices with their start and end apart: 6, of which 4 were waited for; matrix products, arithmetic and copies ran while one was open for 44% of the time, Pallas kernels for 0%

commit v1 on v0

v1 whole, which is shorter than its diff:
```python
import functools

import jax
import jax.numpy as jnp
from jax import lax
from jax.experimental import pallas as pl
from jax.experimental.pallas import tpu as pltpu
from jax.sharding import PartitionSpec as P

HEAD_DIM = 128
SEG = 512
MESH = pl.DeviceIdType.MESH
F32 = jnp.float32
BF16 = jnp.bfloat16
NN = (((1,), (0,)), ((), ()))
NT = (((1,), (1,)), ((), ()))
TN = (((0,), (0,)), ((), ()))


def mm(a, b, dims=NN):
    return lax.dot_general(a, b, dims, preferred_element_type=F32)


def feature(x):
    return jnp.where(x > 0, x + 1.0, jnp.exp(jnp.minimum(x, 0.0)))


def slope(x):
    return jnp.where(x > 0, 1.0, jnp.exp(jnp.minimum(x, 0.0)))


def kernel(
    N, H,
    off_ref, gl_ref, q_ref, k_ref, v_ref, w_ref, gm_ref,
    mixed_ref, dq_ref, dk_ref, dv_ref, dw_ref, dg_ref,
    cot, at, ga, wts, attend, stage, dwin, mem, flow, run, grun, acc,
    m1out, m1in, m2out, m2in,
    ag_s, ag_f, ag_r, mem_s, mem_r, flow_s, flow_r, dw_s, dw_r, m1_s, m1_r, m2_s, m2_r,
):
    X = H // 2
    i = lax.axis_index("ctx")
    h = lax.axis_index("head")
    x, c = lax.div(h, 2), lax.rem(h, 2)
    sibling = {"head": 2 * x + 1 - c}
    heads = q_ref.shape[1] // HEAD_DIM
    groups = k_ref.shape[1] // HEAD_DIM
    repeat = heads // groups
    width = gm_ref.shape[1]
    piece = dw_ref.shape[1]
    per = width // piece
    top = groups * HEAD_DIM
    scale = HEAD_DIM ** (-0.5)

    def ctx_at(d):
        return {"ctx": lax.rem(i + d, N)}

    def x_at(d):
        return {"head": 2 * lax.rem(x + d, X) + c}

    def copy(src, dst, send, recv, device):
        return pltpu.make_async_remote_copy(
            src_ref=src, dst_ref=dst, send_sem=send, recv_sem=recv,
            device_id=device, device_id_type=MESH,
        )

    barrier = pltpu.get_barrier_semaphore()
    for d in range(1, N):
        pl.semaphore_signal(barrier, inc=1, device_id=ctx_at(d), device_id_type=MESH)
    for d in range(1, X):
        pl.semaphore_signal(barrier, inc=1, device_id=x_at(d), device_id_type=MESH)
    pl.semaphore_signal(barrier, inc=1, device_id=sibling, device_id_type=MESH)
    pl.semaphore_wait(barrier, N - 1 + X)

    sends = []
    for d in range(1, X):
        sends.append(copy(gm_ref, cot.at[h], ag_s.at[d], ag_r.at[h], x_at(d)))
    sends.append(copy(gm_ref, cot.at[h], ag_s.at[0], ag_r.at[h], sibling))
    for one in sends:
        one.start()

    o = off_ref[0]
    start = jnp.where(o == SEG, 0, o)
    carry = jnp.where(o == SEG, 1.0, 0.0)
    pos = lax.broadcasted_iota(jnp.int32, (SEG, HEAD_DIM), 0)
    retain = jnp.where(pos < o, 1.0, 0.0)
    counted = jnp.where(pos >= start, 1.0, 0.0)
    row = lax.broadcasted_iota(jnp.int32, (8, HEAD_DIM), 0)
    zero8 = jnp.zeros((8, HEAD_DIM), F32)

    tot = zero8
    for g in range(groups):
        cols = slice(g * HEAD_DIM, (g + 1) * HEAD_DIM)
        kf = feature(k_ref[:, cols].astype(F32)) * counted
        mem[i, cols, :] = mm(kf.astype(BF16), v_ref[:, cols], TN).astype(BF16)
        tot = jnp.where(row == g, jnp.sum(kf, axis=0, keepdims=True), tot)
    tail = jnp.concatenate([tot, jnp.full((8, HEAD_DIM), carry, F32)], axis=0)
    mem[i, top:top + 16, :] = tail.astype(BF16)
    for d in range(1, N):
        one = copy(mem.at[i], mem.at[i], mem_s.at[d], mem_r.at[i], ctx_at(d))
        one.start()
        sends.append(one)

    def lane(n):
        return pl.ds(pl.multiple_of(n * HEAD_DIM, HEAD_DIM), HEAD_DIM)

    def attend_head(n, _):
        g = lax.div(n, repeat)
        s = mm(q_ref[:, lane(n)], k_ref[:, lane(g)], NT) * scale
        qi = lax.broadcasted_iota(jnp.int32, (SEG, SEG), 0)
        kj = lax.broadcasted_iota(jnp.int32, (SEG, SEG), 1)
        allowed = (kj <= qi) & ((qi < o) | (kj >= o))
        s = jnp.where(allowed, s, -1e30)
        e = jnp.exp(s - jnp.max(s, axis=-1, keepdims=True))
        weights = e / jnp.sum(e, axis=-1, keepdims=True)
        wts[n] = weights
        attend[n] = mm(weights.astype(BF16), v_ref[:, lane(g)])
        return 0

    lax.fori_loop(0, heads, attend_head, 0)
    for d in range(1, X):
        owner = 2 * lax.rem(x + X - d, X) + c
        copy(cot.at[owner], cot.at[owner], ag_f.at[d], ag_r.at[owner], sibling).wait_recv()
        one = copy(cot.at[owner], cot.at[owner], ag_f.at[d], ag_r.at[owner], sibling)
        one.start()
        sends.append(one)
    cot[h] = gm_ref[...]
    for d in range(X):
        owner = 2 * lax.rem(x + X - d, X) + 1 - c
        copy(cot.at[owner], cot.at[owner], ag_f.at[0], ag_r.at[owner], sibling).wait_recv()

    acc[...] = jnp.zeros_like(acc)

    def back_project(n, _):
        cols = pl.ds(pl.multiple_of(n * width, 128), width)
        acc[...] += mm(cot[n], w_ref[:, cols], NT)
        return 0

    lax.fori_loop(0, H, back_project, 0)
    ga[...] = acc[...].astype(BF16)

    for d in range(1, N):
        p = lax.rem(i + N - d, N)
        copy(mem.at[p], mem.at[p], mem_s.at[d], mem_r.at[p], ctx_at(d)).wait_recv()
    run[...] = jnp.zeros_like(run)

    def forward_hop(p, _):
        factor = mem[p, top:top + 16, :].astype(F32)[8:9, :]
        run[...] = jnp.where(p < i, factor * run[...] + mem[p].astype(F32), run[...])
        return 0

    lax.fori_loop(0, N - 1, forward_hop, 0)

    grun[...] = jnp.zeros_like(grun)

    def recall_head(n, _):
        g = lax.div(n, repeat)
        rows = pl.ds(pl.multiple_of(g * HEAD_DIM, HEAD_DIM), HEAD_DIM)
        gate = jax.nn.sigmoid(jnp.full((1, HEAD_DIM), gl_ref[n], F32))
        query = q_ref[:, lane(n)].astype(F32)
        qf = feature(query) * retain
        qb = qf.astype(BF16)
        memory = run[rows, :].astype(BF16)
        totals = jnp.sum(jnp.where(row == g, run[top:top + 8, :], 0.0), axis=0, keepdims=True)
        numer = mm(qb, memory)
        inverse = 1.0 / (1.0 + jnp.sum(qf * totals, axis=-1, keepdims=True))
        recall = numer * inverse
        local = attend[n]
        at[:, lane(n)] = (gate * recall + (1.0 - gate) * local).astype(BF16)
        grad = ga[:, lane(n)].astype(F32)
        term = jnp.sum(grad * (recall - local), axis=0, keepdims=True)
        term = jnp.sum(term, axis=1, keepdims=True) * (gate * (1.0 - gate))
        grad_recall = gate * grad
        grad_numer = (grad_recall * inverse).astype(BF16)
        grad_denom = -jnp.sum(grad_recall * numer, axis=-1, keepdims=True) * (inverse * inverse)
        grad_feat = retain * (mm(grad_numer, memory, NT) + grad_denom * totals)
        dq_ref[:, lane(n)] = grad_feat * slope(query)
        grun[rows, :] += mm(qb, grad_numer, TN)
        part = jnp.sum(grad_denom * qf, axis=0, keepdims=True)
        grun[top:top + 8, :] += jnp.where(row == g, part, 0.0)
        grun[top + 8:top + 16, :] += jnp.where(row == n, term, 0.0)
        return 0

    lax.fori_loop(0, heads, recall_head, 0)
    packed = grun[...].astype(BF16)
    flow[i, :top + 16, :] = packed
    gates = grun[top + 8:top + 16, :]
    rest = gates - gates.astype(BF16).astype(F32)
    flow[i, top + 16:top + 32, :] = jnp.concatenate([rest, zero8], axis=0).astype(BF16)
    for d in range(1, N):
        one = copy(flow.at[i], flow.at[i], flow_s.at[d], flow_r.at[i], ctx_at(d))
        one.start()
        sends.append(one)

    def weight_block(n, _):
        block = mm(at[...], cot[n], TN).astype(BF16)
        for j in range(per):
            stage[n * per + j] = block[:, j * piece:(j + 1) * piece]
        return 0

    lax.fori_loop(0, H, weight_block, 0)
    for d in range(1, N):
        one = copy(stage.at[lax.rem(i + d, N)], dwin.at[d - 1], dw_s.at[d], dw_r.at[d], ctx_at(d))
        one.start()
        sends.append(one)

    def partial(xx, cc):
        cols = pl.ds(pl.multiple_of((2 * xx + cc) * width, 128), width)
        return mm(at[...], w_ref[:, cols])

    pair = []
    for d in range(X):
        m1out[d] = partial(lax.rem(x + d, X), 1 - c).astype(BF16)
        one = copy(m1out.at[d], m1in.at[d], m1_s.at[d], m1_r.at[d], sibling)
        one.start()
        pair.append(one)
    far = []
    for d in list(range(1, X)) + [0]:
        mine = partial(lax.rem(x + d, X), c)
        pair[d].wait_recv()
        mine = mine + m1in[d].astype(F32)
        if d:
            m2out[d - 1] = mine.astype(BF16)
            one = copy(m2out.at[d - 1], m2in.at[d - 1], m2_s.at[d], m2_r.at[d], x_at(d))
            one.start()
            far.append(one)
        else:
            acc[...] = mine

    dk_ref[...] = jnp.zeros_like(dk_ref)
    dv_ref[...] = jnp.zeros_like(dv_ref)

    def backward_head(n, _):
        g = lax.div(n, repeat)
        away = 1.0 - jax.nn.sigmoid(jnp.full((1, SEG), gl_ref[n], F32))
        key, value = k_ref[:, lane(g)], v_ref[:, lane(g)]
        grad = ga[:, lane(n)]
        weights = wts[n]
        probs = away * mm(grad, value, NT)
        inner = jnp.sum(probs * weights, axis=-1, keepdims=True)
        low = (weights * (probs - inner) * scale).astype(BF16)
        dq_ref[:, lane(n)] += mm(low, key)
        dk_ref[:, lane(g)] += mm(low, q_ref[:, lane(n)], TN)
        dv_ref[:, lane(g)] += away[:, :HEAD_DIM] * mm(weights.astype(BF16), grad, TN)
        return 0

    lax.fori_loop(0, heads, backward_head, 0)

    total = acc[...]
    for d in range(1, X):
        far[d - 1].wait_recv()
        total = total + m2in[d - 1].astype(F32)
    mixed_ref[...] = total.astype(BF16)

    for d in range(1, N):
        p = lax.rem(i + N - d, N)
        copy(flow.at[p], flow.at[p], flow_s.at[d], flow_r.at[p], ctx_at(d)).wait_recv()
    run[...] = jnp.zeros_like(run)
    dg_ref[...] = zero8

    def backward_hop(t, _):
        p = N - 1 - t
        tail = flow[p, top:top + 32, :].astype(F32)
        dg_ref[...] += tail[8:16, :] + tail[16:24, :]
        factor = mem[p, top:top + 16, :].astype(F32)[8:9, :]
        run[...] = jnp.where(p > i, factor * run[...] + flow[p, :top + 16, :].astype(F32), run[...])
        return 0

    lax.fori_loop(0, N, backward_hop, 0)
    for g in range(groups):
        cols = slice(g * HEAD_DIM, (g + 1) * HEAD_DIM)
        key = k_ref[:, cols].astype(F32)
        memory = run[cols, :].astype(BF16)
        extra = mm(v_ref[:, cols], memory, NT) + run[top + g:top + g + 1, :]
        dk_ref[:, cols] += counted * extra * slope(key)
        dv_ref[:, cols] += counted * mm(feature(key).astype(BF16), memory)

    dw_ref[...] = stage[i].astype(F32)
    for d in range(1, N):
        copy(stage.at[i], dwin.at[d - 1], dw_s.at[d], dw_r.at[d], ctx_at(d)).wait_recv()
        dw_ref[...] += dwin[d - 1].astype(F32)
    for one in sends + pair + far:
        one.wait_send()


def body(N, H, queries, keys, values, offsets, gate_logits, out_weight, grad_mixed):
    tokens, qw = queries.shape
    kw = keys.shape[1]
    rows, out_cols = out_weight.shape
    width = grad_mixed.shape[1]
    heads = qw // HEAD_DIM
    piece = out_cols // N
    X = H // 2
    top = kw
    vm = pl.BlockSpec(memory_space=pltpu.VMEM)
    sm = pl.BlockSpec(memory_space=pltpu.SMEM)
    dma = pltpu.SemaphoreType.DMA
    far = max(X - 1, 1)
    out = pl.pallas_call(
        functools.partial(kernel, N, H),
        out_shape=(
            jax.ShapeDtypeStruct((tokens, width), BF16),
            jax.ShapeDtypeStruct((tokens, qw), F32),
            jax.ShapeDtypeStruct((tokens, kw), F32),
            jax.ShapeDtypeStruct((tokens, kw), F32),
            jax.ShapeDtypeStruct((rows, piece), F32),
            jax.ShapeDtypeStruct((8, HEAD_DIM), F32),
        ),
        in_specs=[sm, sm] + [vm] * 5,
        out_specs=(vm,) * 6,
        scratch_shapes=[
            pltpu.VMEM((H, tokens, width), BF16),
            pltpu.VMEM((tokens, qw), BF16),
            pltpu.VMEM((tokens, qw), BF16),
            pltpu.VMEM((heads, SEG, SEG), F32),
            pltpu.VMEM((heads, SEG, HEAD_DIM), F32),
            pltpu.VMEM((N, rows, piece), BF16),
            pltpu.VMEM((N - 1, rows, piece), BF16),
            pltpu.VMEM((N, top + 16, HEAD_DIM), BF16),
            pltpu.VMEM((N, top + 32, HEAD_DIM), BF16),
            pltpu.VMEM((top + 16, HEAD_DIM), F32),
            pltpu.VMEM((top + 16, HEAD_DIM), F32),
            pltpu.VMEM((tokens, max(width, qw)), F32),
            pltpu.VMEM((X, tokens, width), BF16),
            pltpu.VMEM((X, tokens, width), BF16),
            pltpu.VMEM((far, tokens, width), BF16),
            pltpu.VMEM((far, tokens, width), BF16),
            dma((X,)), dma((X,)), dma((H,)),
            dma((N,)), dma((N,)), dma((N,)), dma((N,)), dma((N,)), dma((N,)),
            dma((X,)), dma((X,)), dma((X,)), dma((X,)),
        ],
        compiler_params=pltpu.CompilerParams(
            collective_id=0, has_side_effects=True, vmem_limit_bytes=56 * 1024 * 1024
        ),
    )(offsets, gate_logits, queries, keys, values, out_weight, grad_mixed)
    return (*out[:5], out[5][:heads, 0])


def solution(mesh):
    placed = (
        P("ctx", "head"),
        P("ctx", "head"),
        P("ctx", "head"),
        P("ctx"),
        P("head"),
        P("head", None),
        P("ctx", "head"),
    )
    return jax.shard_map(
        functools.partial(body, mesh.shape["ctx"], mesh.shape["head"]),
        mesh=mesh,
        in_specs=placed,
        out_specs=(
            P("ctx", "head"),
            P("ctx", "head"),
            P("ctx", "head"),
            P("ctx", "head"),
            P("head", "ctx"),
            P("head"),
        ),
        check_vma=False,
    )
```

time: 248 us -> 94.5 us (0.38); the launches traced: 245 us -> 94.3 us
  Pallas kernels: 0 us -> 85 us
  blocking collectives: 58.1 us -> 0 us
  waiting for transfers between devices: 51.3 us -> 0 us
  matrix products: 41.6 us -> 0 us
  other arithmetic: 39.4 us -> 0 us
  local copies, waits for them, and re-layouts: 35 us -> 8 us
  between operations: 14.8 us -> 1.3 us
  starting transfers between devices: 4.72 us -> 0 us
    pallas_call x0 -> x1, Pallas kernels: none -> 85 us  [body(): pl.pallas_call(functools.partial(kernel, N, H), out_shape=(jax.ShapeDtype...]
    dot_general x17 -> x0, matrix products: 41.6 us -> none  [the longest x1 4.98 us: body(): lax.dot_general(out_flat, cotangent, (((0,), (0,)), ((), ())), preferred_...]
    select_n x30 -> x0, other arithmetic: 35.8 us -> none  [the longest x28 31.7 us: hop(): jnp.where(position < mine, new, old)]
    reduce_scatter x1 -> x0, waiting for transfers between devices: 31.9 us -> none  [body(): lax.psum_scatter(weight_terms, 'ctx', scatter_dimension=1, tiled=True)]
    all_gather x2 -> x0, blocking collectives: 25.5 us -> none  [carried_in(): pieces = jax.tree.map(lambda part: lax.all_gather(part, axis), value)]
    unnamed x1 -> x0, blocking collectives: 18.1 us -> none
    psum x1 -> x0, blocking collectives: 14.5 us -> none  [body(): grad_gates = lax.psum(gate_terms, 'ctx')]
    dynamic_slice x14 -> x0, local copies, waits for them, and re-layouts: 12.6 us -> none  [hop(): longer = join(running, jax.tree.map(lambda part: part[position], pieces))]
  transfers between devices with their start and end apart: 6 -> 0, of which waited for: 4 -> 0; matrix products, arithmetic and copies ran while one was open for 44% -> 0% of each run, Pallas kernels for 0% -> 0%
where the time goes in v1:
time: 94.5 us; the launch traced here: 94.3 us
  Pallas kernels  85 us (90%)
  local copies, waits for them, and re-layouts  8 us (8%)
  between operations  1.3 us (1%)
    pallas_call x1, Pallas kernels, body(): pl.pallas_call(functools.partial(kernel, N, H), out_shape=(jax.ShapeDtype...  85 us
    unnamed x11, local copies, waits for them, and re-layouts  6.64 us

profile of v1, /device:TPU:13, one launch (start us, length us, event | category | flops | bytes accessed | tf_op | source)
XLA Modules:
  0.0 94.3 jit_solution(10351183154665095896)
XLA Ops:
  1.3 85.0 %shard_map.118 = (bf16[512,512]{1,0:T(8,128)(2,1)}, f32[512,512]{1,0:T(8,128)}, f32[512,256]{1,0:T(8,128)}, f32[512,256]{1,0:T(8,128)}, f32[512,256]{1,0:T(8,128)}, /*index=5*/f32[8,128]{1,0:T(8,128)}) custom-call(s32[1]{0:T(128)S(6)} %copy.18.off_ref, f32[4]{0:T(128)} %gl_ref.1, bf16[512,512]{1,0:T(8,128)(2,1)} %q_ref.1, bf16[512,256]{1,0:T(8,128)(2,1)} %k_ref.1, ...), custom_call_target="tpu_custom_call" | custom-call | tf_op jit(solution)/shard_map/pallas_call | solution.py:298
  86.3 0.0 copy-start.2
  86.3 1.4 %slice_reduce_fusion = f32[4]{0:T(128)} fusion(f32[8,128]{1,0:T(8,128)} %get-tuple-element.17), kind=kLoop, calls=%fused_computation | loop fusion | bytes 32 | tf_op jit(solution)/shard_map/slice | solution.py:335
  87.7 0.0 copy-start.1
  87.7 1.9 %copy.19 = bf16[512,512]{1,0:T(8,128)(2,1)} copy(bf16[512,512]{1,0:T(8,128)(2,1)} %get-tuple-element.24) | data formatting | bytes 1048576
  89.6 0.0 copy-start
  89.6 2.3 %copy.20 = f32[512,512]{1,0:T(8,128)} copy(f32[512,512]{1,0:T(8,128)} %get-tuple-element.25) | data formatting | bytes 2097152
  91.9 0.0 copy-done.2
  91.9 0.8 copy.21
  92.7 0.0 copy-done.1
  92.7 0.8 copy.22
  93.5 0.0 copy-done
  93.5 0.8 copy.23
Async XLA Ops:
  86.3 5.6 %copy-start.2 = (f32[512,256]{1,0:T(8,128)S(1)}, f32[512,256]{1,0:T(8,128)}, u32[]{:S(2)}) copy-start(f32[512,256]{1,0:T(8,128)} %get-tuple-element.26) | copy-start | bytes 1572868
  87.7 5.0 %copy-start.1 = (f32[512,256]{1,0:T(8,128)S(1)}, f32[512,256]{1,0:T(8,128)}, u32[]{:S(2)}) copy-start(f32[512,256]{1,0:T(8,128)} %get-tuple-element.27) | copy-start | bytes 1572868
  89.6 3.9 %copy-start = (f32[512,256]{1,0:T(8,128)S(1)}, f32[512,256]{1,0:T(8,128)}, u32[]{:S(2)}) copy-start(f32[512,256]{1,0:T(8,128)} %get-tuple-element.28) | copy-start | bytes 1572868
